TPU v7x, 256 devices: a whole 4x4x8 slice. The times are simulated.
256 devices in a mesh: req: 8 (over y, core), mp: 32 (over z, x).
Axes of the slice: x: 4, y: 4, z: 8, core: 2. Of those that a mesh axis runs over, the one named last changes fastest.
Arguments:
- draft_hidden: bfloat16 [16, 2048], P('req'), may hold values from -6 to 6
- draft_weight: bfloat16 [4, 2048, 2048], P(None, None, 'mp'), may hold values from -0.125 to 0.125
- vocab_weight: bfloat16 [98304, 2048], P(('req', 'mp')), may hold values from -0.375 to 0.375
- tree_inputs: bfloat16 [768, 2048], P('req')
- tree_parent: int32 [16, 48], P('req'), may hold values from -1 to 41, as said below
- cache_len: int32 [16], P('req'), may hold values from 1 to 8192, as said below
- page_table: int32 [16, 64], P('req'), may hold values from -1 to 1023, as said below
- kv_cache: bfloat16 [1024, 2, 128, 2048], P(('req', 'mp'))
- accepted_node: int32 [16], P('req'), may hold values from 0 to 47
- qkv_weight: bfloat16 [2048, 3, 2048], P(None, None, 'mp'), may hold values from -0.125 to 0.125
- norm_gains: bfloat16 [4, 2048], replicated, may hold values from 0.5 to 1.5
- out_weight: bfloat16 [2048, 2048], P(None, 'mp'), may hold values from -0.125 to 0.125
- gate_up_weight: bfloat16 [2048, 2, 8192], P(None, None, 'mp'), may hold values from -0.125 to 0.125
- down_weight: bfloat16 [8192, 2048], P('mp'), may hold values from -0.0625 to 0.0625
Outputs:
- draft_logits: float32 [16, 4, 98304], P(None, None, ('req', 'mp'))
- layer_out: bfloat16 [768, 2048], P(('req', 'mp'))
- accepted_kv: bfloat16 [16, 4, 2, 2048], P('req', None, None, 'mp')
Inputs may be any that keep to these rules, and one draw needn't show every extreme that they name: `page_table`: row r lists the pool pages of request r in the order of its tokens, ceil(cache_len[r] / 128) of them, then -1. The pages of the requests of one index of req lie in that index's part of kv_cache, and no page serves two requests. `cache_len`: on every index of req some request has exactly 8192 cached tokens. `tree_parent`: A parent has a smaller index than its child; a node has at most 3 ancestors.
All inputs are finite; a program needn't handle non-finite values.
Results may differ from a plain program's by a relative error of at most 0.01355.
Values may be sent and summed in bfloat16 or wider, within the bound.
No kernel may reach another device: no remote copies, remote signals or barrier semaphores. Data moves between devices by JAX's collectives and lax.ppermute only.
A program may use at most 128 MiB of HBM per device.

v0:
```python
import jax
import jax.numpy as jnp
from jax import lax
from jax.sharding import PartitionSpec as P

HEADS = 16
HEAD_DIM = 128
rope_base = 500000.0
norm_epsilon = 1e-06
masked_score = -1e30


def combined_all(part, axis, combine):
    gathered = jax.tree.map(lambda a: lax.all_gather(a, axis), part)

    def take(source):
        return jax.tree.map(lambda a: lax.dynamic_index_in_dim(a, source, 0, False), gathered)

    return lax.fori_loop(
        1, lax.axis_size(axis), lambda source, state: combine(state, take(source)), take(0)
    )


def rms_scaled(entries, gain_row):
    mean_square = jnp.mean(entries * entries, axis=-1, keepdims=True)
    return entries * lax.rsqrt(mean_square + norm_epsilon) * gain_row


def tree_shape(parents):
    node_count = parents.shape[-1]
    step_one = (
        parents[..., :, None] == jnp.arange(node_count, dtype=jnp.int32)[None, None, :]
    ).astype(jnp.float32)
    step_two = jnp.einsum("rij,rjk->rik", step_one, step_one, precision=lax.Precision.HIGHEST)
    step_three = jnp.einsum("rij,rjk->rik", step_two, step_one, precision=lax.Precision.HIGHEST)
    ancestry = jnp.eye(node_count, dtype=jnp.float32)[None] + step_one + step_two + step_three
    return (ancestry, jnp.sum(ancestry, axis=-1))


def rotate(entries, positions):
    row_count = entries.shape[0]
    half_dim = HEAD_DIM // 2
    shaped = entries.reshape(row_count, HEADS, HEAD_DIM)
    freqs = rope_base ** (-jnp.arange(half_dim, dtype=jnp.float32) * 2.0 / HEAD_DIM)
    angles = positions[:, None] * freqs[None, :]
    cosine = jnp.cos(angles)[:, None, :]
    sine_part = jnp.sin(angles)[:, None, :]
    front = shaped[..., :half_dim]
    back_half = shaped[..., half_dim:]
    turned = jnp.concatenate(
        [front * cosine - back_half * sine_part, back_half * cosine + front * sine_part], axis=-1
    )
    return turned.reshape(row_count, HEADS * HEAD_DIM)


def fold_states(left_state, right_state):
    top_left, total_left, mixed_left = left_state
    top_right, total_right, mixed_right = right_state
    top_both = jnp.maximum(top_left, top_right)
    factor_left = jnp.exp(top_left - top_both)
    factor_right = jnp.exp(top_right - top_both)
    return (
        top_both,
        total_left * factor_left + total_right * factor_right,
        mixed_left * factor_left[..., None] + mixed_right * factor_right[..., None],
    )


def tree_states(query_part, key_part, value_part, ancestry):
    scale = HEAD_DIM ** (-0.5)
    scores = (
        jnp.einsum("rthe,rshe->rths", query_part, key_part, preferred_element_type=jnp.float32)
        * scale
    )
    visible = (ancestry > 0.5)[:, :, None, :]
    scores = jnp.where(visible, scores, masked_score)
    top_score = jnp.max(scores, axis=-1)
    weights = jnp.where(visible, jnp.exp(scores - top_score[..., None]), 0.0)
    totals = jnp.sum(weights, axis=-1)
    mixed = jnp.einsum(
        "rths,rshe->rthe",
        weights.astype(jnp.bfloat16),
        value_part,
        preferred_element_type=jnp.float32,
    )
    return (top_score, totals, mixed)


def page_states(queries, cache_len, page_table, kv_cache, first_slot):
    scale = HEAD_DIM ** (-0.5)
    page_count = kv_cache.shape[0]
    page_len = kv_cache.shape[2]
    table_width = page_table.shape[1]
    req_local = page_table.shape[0]
    slots = first_slot + jnp.arange(page_count, dtype=jnp.int32)
    matches = page_table[None, :, :] == slots[:, None, None]
    owner_hot = jnp.any(matches, axis=2)
    page_index = jnp.sum(
        jnp.where(matches, jnp.arange(table_width, dtype=jnp.int32)[None, None, :], 0), axis=(1, 2)
    )
    owner = jnp.sum(
        jnp.where(matches, jnp.arange(req_local, dtype=jnp.int32)[None, :, None], 0), axis=(1, 2)
    )
    in_use = jnp.any(matches, axis=(1, 2))
    limit = jnp.take(cache_len, owner)
    token_pos = page_index[:, None] * page_len + jnp.arange(page_len, dtype=jnp.int32)[None, :]
    valid = in_use[:, None] & (token_pos < limit[:, None])
    page_keys = kv_cache[:, 0].reshape(page_count, page_len, HEADS, HEAD_DIM)
    page_values = kv_cache[:, 1].reshape(page_count, page_len, HEADS, HEAD_DIM)
    asked = jnp.take(queries, owner, axis=0)
    scores = (
        jnp.einsum("pthe,pshe->phts", asked, page_keys, preferred_element_type=jnp.float32) * scale
    )
    visible = valid[:, None, None, :]
    scores = jnp.where(visible, scores, masked_score)
    top_score = jnp.max(scores, axis=-1)
    weights = jnp.where(visible, jnp.exp(scores - top_score[..., None]), 0.0)
    totals = jnp.sum(weights, axis=-1)
    mixed = jnp.einsum(
        "phts,pshe->pthe",
        weights.astype(jnp.bfloat16),
        page_values,
        preferred_element_type=jnp.float32,
    )
    owner_mask = owner_hot[:, :, None, None]
    top_request = jnp.max(jnp.where(owner_mask, top_score[:, None], masked_score), axis=0)
    spread_gap = jnp.where(owner_mask, top_score[:, None] - top_request[None], 0.0)
    factor = jnp.where(owner_mask, jnp.exp(spread_gap), 0.0)
    total_request = jnp.sum(factor * totals[:, None], axis=0)
    mixed_request = jnp.einsum("prht,pthe->rthe", factor, mixed, precision=lax.Precision.HIGHEST)
    return (
        jnp.transpose(top_request, (0, 2, 1)),
        jnp.transpose(total_request, (0, 2, 1)),
        mixed_request,
    )


def per_device(
    draft_hidden,
    draft_weight,
    vocab_weight,
    tree_inputs,
    tree_parent,
    cache_len,
    page_table,
    kv_cache,
    accepted_node,
    qkv_weight,
    norm_gains,
    out_weight,
    gate_up_weight,
    down_weight,
):
    mp_count = lax.axis_size("mp")
    req_count = lax.axis_size("req")
    mp_place = lax.axis_index("mp")
    req_place = lax.axis_index("req")
    req_local = draft_hidden.shape[0]
    model_width = draft_hidden.shape[1]
    draft_count = draft_weight.shape[0]
    slab_width = draft_weight.shape[2]
    vocab_local = vocab_weight.shape[0]
    draft_raw = jnp.einsum(
        "rd,kde->rke", draft_hidden, draft_weight, preferred_element_type=jnp.float32
    )
    own_columns = lax.dynamic_slice_in_dim(
        draft_hidden, mp_place * slab_width, slab_width, 1
    ).astype(jnp.float32)
    drafted = (own_columns[:, None, :] + jax.nn.silu(draft_raw)).astype(jnp.bfloat16)
    collected = lax.all_gather(drafted[None], ("req", "mp"), axis=0, tiled=True)
    collected = collected.reshape(req_count, mp_count, req_local, draft_count, slab_width)
    vocab_table = vocab_weight.reshape(vocab_local, mp_count, slab_width)
    draft_logits = jnp.einsum(
        "gmrkc,vmc->grkv", collected, vocab_table, preferred_element_type=jnp.float32
    ).reshape(req_count * req_local, draft_count, vocab_local)
    row_count = tree_inputs.shape[0]
    tree_size = tree_parent.shape[1]
    own_projection = jnp.einsum(
        "td,dce->tce", tree_inputs, qkv_weight, preferred_element_type=jnp.float32
    ).astype(jnp.bfloat16)
    projected = lax.all_gather(own_projection, "mp", axis=2, tiled=True)
    ancestry, node_depth = tree_shape(tree_parent)
    positions = (cache_len[:, None].astype(jnp.float32) + node_depth - 1.0).reshape(row_count)
    gain_rows = norm_gains.astype(jnp.float32)
    queries = (
        rotate(rms_scaled(projected[:, 0].astype(jnp.float32), gain_rows[0]), positions)
        .astype(jnp.bfloat16)
        .reshape(req_local, tree_size, HEADS, HEAD_DIM)
    )
    keys_tree = (
        rotate(rms_scaled(projected[:, 1].astype(jnp.float32), gain_rows[1]), positions)
        .astype(jnp.bfloat16)
        .reshape(req_local, tree_size, HEADS, HEAD_DIM)
    )
    values_tree = projected[:, 2].reshape(req_local, tree_size, HEADS, HEAD_DIM)
    chosen = (accepted_node[:, None] == jnp.arange(tree_size, dtype=jnp.int32)[None, :]).astype(
        jnp.float32
    )
    on_path = jnp.einsum("rt,rts->rs", chosen, ancestry, precision=lax.Precision.HIGHEST)
    levels = jnp.arange(1, draft_count + 1, dtype=jnp.float32)
    picker = on_path[:, None, :] * (node_depth[:, None, :] == levels[None, :, None]).astype(
        jnp.float32
    )
    key_columns = lax.dynamic_slice_in_dim(
        keys_tree.reshape(req_local, tree_size, model_width), mp_place * slab_width, slab_width, 2
    )
    value_columns = own_projection[:, 2].reshape(req_local, tree_size, slab_width)
    stacked = jnp.stack([key_columns, value_columns], axis=2)
    accepted_kv = jnp.einsum(
        "rjs,rsce->rjce", picker.astype(jnp.bfloat16), stacked, preferred_element_type=jnp.float32
    ).astype(jnp.bfloat16)
    first_slot = (req_place * mp_count + mp_place) * kv_cache.shape[0]
    page_part = page_states(queries, cache_len, page_table, kv_cache, first_slot)
    identity = (
        jnp.full((req_local, tree_size, HEADS), masked_score, jnp.float32),
        jnp.zeros((req_local, tree_size, HEADS), jnp.float32),
        jnp.zeros((req_local, tree_size, HEADS, HEAD_DIM), jnp.float32),
    )
    tree_part = lax.cond(
        mp_place == 0,
        lambda: tree_states(queries, keys_tree, values_tree, ancestry),
        lambda: identity,
    )
    local_state = fold_states(page_part, tree_part)
    merged = combined_all(local_state, "mp", fold_states)
    attended = (
        (merged[2] / merged[1][..., None]).astype(jnp.bfloat16).reshape(row_count, model_width)
    )
    out_columns = jnp.dot(attended, out_weight, preferred_element_type=jnp.float32).astype(
        jnp.bfloat16
    )
    projected_out = lax.all_gather(out_columns, "mp", axis=1, tiled=True)
    residual = (
        tree_inputs.astype(jnp.float32)
        + rms_scaled(projected_out.astype(jnp.float32), gain_rows[2])
    ).astype(jnp.bfloat16)
    gate_up = jnp.einsum(
        "td,dce->tce", residual, gate_up_weight, preferred_element_type=jnp.float32
    )
    hidden = (jax.nn.silu(gate_up[:, 0]) * gate_up[:, 1]).astype(jnp.bfloat16)
    row_share = row_count // mp_count
    first_row = mp_place * row_share
    summed = lax.psum(
        jnp.dot(hidden, down_weight, preferred_element_type=jnp.float32).astype(jnp.bfloat16), "mp"
    ).astype(jnp.float32)
    own_rows = lax.dynamic_slice_in_dim(summed, first_row, row_share, 0)
    residual_rows = lax.dynamic_slice_in_dim(residual, first_row, row_share, 0).astype(jnp.float32)
    layer_out = (residual_rows + rms_scaled(own_rows, gain_rows[3])).astype(jnp.bfloat16)
    return (draft_logits, layer_out, accepted_kv)


def solution(mesh):
    placed = (
        P("req", None),
        P(None, None, "mp"),
        P(("req", "mp"), None),
        P("req", None),
        P("req", None),
        P("req"),
        P("req", None),
        P(("req", "mp"), None, None, None),
        P("req"),
        P(None, None, "mp"),
        P(),
        P(None, "mp"),
        P(None, None, "mp"),
        P("mp", None),
    )
    return jax.shard_map(
        per_device,
        mesh=mesh,
        in_specs=placed,
        out_specs=(
            P(None, None, ("req", "mp")),
            P(("req", "mp"), None),
            P("req", None, None, "mp"),
        ),
        check_vma=False,
    )
```

profile of v0, /device:TPU:8, one launch (start us, length us, event | category | flops | bytes accessed | tf_op | source)
XLA Modules:
  0.0 613.0 jit_solution(11031418135957718343)
XLA Ops:
  7.2 1.7 fusion.81
  13.2 4.8 fusion.77
  18.1 4.0 copy.281
  22.0 4.0 copy.280
  27.2 64.1 %all-gather.7.cloned.1.call-done = bf16[96,3,2048]{0,2,1:T(8,128)(2,1)} async-done(((bf16[96,3,64]{0,2,1:T(8,128)(2,1)}), bf16[96,3,2048]{0,2,1:T(8,128)(2,1)}) %all-gather.7.cloned.1.call-update) | async-done | bytes 1179664 | tf_op jit(solution)/shard_map/all_gather | solution.py:181
  91.3 2.3 slice_convert_fusion.1
  93.6 2.5 copy.242
  103.2 3.5 fusion.80
  107.0 2.4 fusion.20
  109.4 4.4 convolution_bitcast_fusion.1
  115.9 8.8 %fusion.17 = f32[48,16,128,2]{2,3,1,0:T(2,128)} fusion(f32[4,48,16,128]{3,1,2,0:T(8,128)} %convolution_bitcast_fusion.1, pred[4,2]{0,1:T(4,128)(4,1)S(1)} %get-tuple-element.271, f32[2,16,48]{0,1,2:T(8,128)S(1)} %select_reduce_fusion, f32[4,16,48]{0,1,2:T(8,128)S(1)} %copy.248), kind=kOutput, calls=%fused_computation.29 | convolution fusion | flops 9455616 | bytes 2377736 | tf_op jit(solution)/shard_map/prht,pthe->rthe/dot_general | solution.py:130
  124.7 2.8 multiply_reduce_fusion.2
  128.7 2.1 pad_maximum_fusion
  130.8 7.8 %conditional.1 = (f32[2,48,16]{1,2,0:T(8,128)}, f32[2,48,16]{1,2,0:T(8,128)S(1)}, f32[2,48,16,128]{3,2,1,0:T(8,128)S(1)}) conditional(s32[]{:T(128)} %convert_element_type.124, () %tuple.38, (f32[2,48,48]{1,2,0:T(8,128)S(1)}, bf16[96,16,128]{2,1,0:T(8,128)(2,1)}, bf16[2,48,16,128]{3,2,1,0:T(8,128)(2,1)S(1)}, bf16[96,3,2048]{0,2,1:T(8,128)(2,1)}) %tuple.104), branch_computations={%region_9.10_spmd, %region_10.13_spmd} | conditional | flops 38413824 | bytes 8417304 | solution.py:219
  130.8 2.5 copy.252
  134.4 2.0 fusion.76
  140.1 2.5 fusion.26
  144.2 1.7 fusion.54
  146.0 69.4 %all-gather = bf16[512,4,64]{2,1,0:T(4,128)(2,1)S(1)} all-gather(bf16[2,4,64]{2,1,0:T(4,128)(2,1)S(1)} %add_convert_fusion.1), channel_id=2, replica_groups=mesh['req'=8,'mp'=32] {'req','mp'}, dimensions={0}, use_global_device_ids=true | all-gather | bytes 263168 | tf_op jit(solution)/shard_map/all_gather | solution.py:170
  215.8 2.7 copy.241
  218.5 1.8 convolution_bitcast_fusion.2
  221.9 46.9 %all-gather.2 = f32[64,48,16]{1,2,0:T(8,128)S(1)} all-gather(f32[2,48,16]{1,2,0:T(8,128)S(1)} %copy-done.9), channel_id=4, replica_groups=mesh['req'=8,'mp'=32] {'mp'}, dimensions={0}, use_global_device_ids=true | all-gather | bytes 202752 | tf_op jit(solution)/shard_map/all_gather | solution.py:14
  268.7 50.1 %all-gather.1 = f32[64,48,16]{1,2,0:T(8,128)S(1)} all-gather(f32[2,48,16]{1,2,0:T(8,128)S(1)} %get-tuple-element.307), channel_id=3, replica_groups=mesh['req'=8,'mp'=32] {'mp'}, dimensions={0}, use_global_device_ids=true | all-gather | bytes 202752 | tf_op jit(solution)/shard_map/all_gather | solution.py:14
  319.7 6.9 %all-gather.9.cloned.1.call-done = f32[64,48,16,128]{3,2,1,0:T(8,128)} async-done(((f32[2,48,16,128]{3,2,1,0:T(8,128)}), f32[64,48,16,128]{3,2,1,0:T(8,128)}) %all-gather.9.cloned.1.call-update) | async-done | bytes 25165840 | tf_op jit(solution)/shard_map/all_gather | solution.py:14
  327.7 80.2 %while.19 = (s32[]{:T(128)}, f32[2,48,16]{1,2,0:T(8,128)S(1)}, f32[2,48,16]{1,2,0:T(8,128)S(1)}, f32[2,48,16,128]{3,2,1,0:T(8,128)S(1)}, f32[32,2,48,16]{2,3,1,0...) while((s32[]{:T(128)}, f32[2,48,16]{1,2,0:T(8,128)S(1)}, ...), condition=%wide.region_16.17_spmd, body=%wide.region_15.16_spmd.sunk | while | flops 599045 | bytes 2445455 | solution.py:19
  328.7 1.7 fusion.96
  331.2 1.7 fusion.96
  333.8 1.7 fusion.96
  336.4 1.7 fusion.96
  339.0 1.7 fusion.96
  341.6 1.7 fusion.96
  344.2 1.7 fusion.96
  346.8 1.7 fusion.96
  349.4 1.7 fusion.96
  352.0 1.7 fusion.96
  354.5 1.7 fusion.96
  357.1 1.7 fusion.96
  359.7 1.7 fusion.96
  362.3 1.7 fusion.96
  364.9 1.7 fusion.96
  367.5 1.7 fusion.96
  383.0 1.7 fusion.96
  385.6 1.7 fusion.96
  388.2 1.7 fusion.96
  390.8 1.7 fusion.96
  393.4 1.7 fusion.96
  409.6 47.5 %all_gather.35 = bf16[96,2048]{0,1:T(8,128)(2,1)S(1)} all-gather(bf16[96,64]{0,1:T(8,128)(2,1)S(1)} %convolution_convert_fusion.1), channel_id=1, replica_groups=mesh['req'=8,'mp'=32] {'mp'}, dimensions={1}, use_global_device_ids=true | all-gather | bytes 405504 | tf_op jit(solution)/shard_map/all_gather | solution.py:232
  462.2 141.7 %all-reduce.2.cloned.1.call-done = bf16[96,2048]{1,0:T(8,128)(2,1)} async-done(((bf16[96,2048]{1,0:T(8,128)(2,1)}), bf16[96,2048]{1,0:T(8,128)(2,1)}) %all-reduce.2.cloned.1.call-update) | async-done | bytes 393232 | tf_op jit(solution)/shard_map/psum | solution.py:243
  (219 shorter events, 79.9 us)
Async XLA Ops:
  7.2 450.6 %copy-start = (bf16[2048,2,256]{2,1,0:T(2,128)(2,1)S(1)}, bf16[2048,2,256]{2,1,0:T(2,128)(2,1)}, u32[]{:S(2)}) copy-start(bf16[2048,2,256]{2,1,0:T(2,128)(2,1)} %param.30) | copy-start | bytes 6291460
  7.2 5.2 copy-start.1
  7.2 5.0 copy-start.14
  7.2 84.1 %all-gather.7.cloned.1.call-start = ((), (), s32[]{:S(2)}) async-start(), calls=%async_computation | async-start | bytes 1622016 | tf_op jit(solution)/shard_map/all_gather | solution.py:181
  9.7 316.9 %all-gather.9.cloned.1.call-start = ((), (), s32[]{:S(2)}) async-start(), calls=%async_computation.2 | async-start | bytes 25952256 | tf_op jit(solution)/shard_map/all_gather | solution.py:14
  12.4 5.7 copy-start.15
  22.0 4.0 copy-start.17
  22.0 4.6 copy-start.8
  97.4 2.9 copy-start.3
  107.0 2.4 copy-start.2
  115.9 8.8 %copy-start.5 = (f32[4,16,48]{0,1,2:T(8,128)S(1)}, f32[4,16,48]{0,1,2:T(8,128)}, u32[]{:S(2)}) copy-start(f32[4,16,48]{0,1,2:T(8,128)} %copy.253) | copy-start | bytes 36868
  140.1 4.0 copy-start.13
  142.7 461.2 %all-reduce.2.cloned.1.call-start = ((), (), s32[]{:S(2)}) async-start(), calls=%async_computation.1 | async-start | bytes 786432 | tf_op jit(solution)/shard_map/psum | solution.py:243
  218.5 2.5 copy-start.19
  218.5 3.3 copy-start.9
  318.8 0.8 copy-start.7
  408.3 49.2 %copy-start.4 = (bf16[96,2048]{1,0:T(8,128)(2,1)S(1)}, bf16[96,2048]{1,0:T(8,128)(2,1)}, u32[]{:S(2)}) copy-start(bf16[96,2048]{1,0:T(8,128)(2,1)} %param.21) | copy-start | bytes 1179652
  408.4 49.2 %copy-start.10 = (f32[1,2048]{1,0:T(1,128)S(1)}, f32[1,2048]{1,0:T(1,128)}, u32[]{:S(2)}) copy-start(f32[1,2048]{1,0:T(1,128)} %get-tuple-element.308) | copy-start | bytes 24580
  457.8 1.2 copy-start.6
  459.0 2.4 copy-start.12
  459.0 2.4 copy-start.16
  459.0 2.4 copy-start.18
  459.0 145.8 %copy-start.11 = (f32[1,2048]{1,0:T(1,128)S(1)}, f32[1,2048]{1,0:T(1,128)}, u32[]{:S(2)}) copy-start(f32[1,2048]{1,0:T(1,128)} %get-tuple-element.311) | copy-start | bytes 24580
Sparse Core Ops, SparseCore 0:
  11.2 80.0 all-gather.6
  142.8 183.7 all-gather.8
  460.3 143.5 all-reduce.1
where the time goes:
time: 617 us; the launch traced here: 613 us
  blocking collectives  214 us (35%)
  waiting for transfers between devices  213 us (35%)
  other arithmetic  101 us (16%)
  local copies, waits for them, and re-layouts  40.3 us (7%)
  matrix products  29.8 us (5%)
  between operations  14.1 us (2%)
    psum x1, waiting for transfers between devices, per_device(): lax.psum(jnp.dot(hidden, down_weight, preferred_element_type=jnp.float32)...  142 us
    all_gather x2, blocking collectives, combined_all(): gathered = jax.tree.map(lambda a: lax.all_gather(a, axis), part)  97 us
    all_gather x1, blocking collectives, per_device(): collected = lax.all_gather(drafted[None], ('req', 'mp'), axis=0, tiled=True)  69.4 us
    all_gather x1, waiting for transfers between devices, per_device(): projected = lax.all_gather(own_projection, 'mp', axis=2, tiled=True)  64.1 us
    add x32, other arithmetic, fold_states(): mixed_left * factor_left[..., None] + mixed_right * factor_right[..., None]  54 us
    all_gather x1, blocking collectives, per_device(): projected_out = lax.all_gather(out_columns, 'mp', axis=1, tiled=True)  47.5 us
    add x32, other arithmetic, fold_states(): total_left * factor_left + total_right * factor_right  24.4 us
    unnamed x45, local copies, waits for them, and re-layouts  13.6 us
  transfers between devices with their start and end apart: 3, of which 3 were waited for; matrix products, arithmetic and copies ran while one was open for 5% of the time, Pallas kernels for 0%

commit v1 on v0

--- a/solution.py
+++ b/solution.py
@@ -240,8 +240,12 @@
     hidden = (jax.nn.silu(gate_up[:, 0]) * gate_up[:, 1]).astype(jnp.bfloat16)
     row_share = row_count // mp_count
     first_row = mp_place * row_share
-    summed = lax.psum(
-        jnp.dot(hidden, down_weight, preferred_element_type=jnp.float32).astype(jnp.bfloat16), "mp"
+    summed = jnp.sum(
+        jax.lax.all_gather(
+            jnp.dot(hidden, down_weight, preferred_element_type=jnp.float32).astype(jnp.bfloat16),
+            axis_name="mp",
+        ),
+        axis=0,
     ).astype(jnp.float32)
     own_rows = lax.dynamic_slice_in_dim(summed, first_row, row_share, 0)
     residual_rows = lax.dynamic_slice_in_dim(residual, first_row, row_share, 0).astype(jnp.float32)

time: 617 us -> 597 us (0.968)
  waiting for transfers between devices: 213 us -> 188 us
  other arithmetic: 101 us -> 108 us
    psum x1 -> x0, waiting for transfers between devices: 142 us -> none  [per_device(): lax.psum(jnp.dot(hidden, down_weight, preferred_element_type=jnp.float32)...]
    all_gather x1, waiting for transfers between devices: 6.87 us -> 84.5 us  [combined_all(): gathered = jax.tree.map(lambda a: lax.all_gather(a, axis), part)]
    all_gather x0 -> x1, waiting for transfers between devices: none -> 39.2 us  [per_device(): jax.lax.all_gather(jnp.dot(hidden, down_weight, preferred_element_type=jn...]
    reduce_sum x0 -> x1, other arithmetic: none -> 7.86 us  [per_device(): jnp.sum(jax.lax.all_gather(jnp.dot(hidden, down_weight, preferred_element...]
    unnamed x45 -> x47, local copies, waits for them, and re-layouts: 13.6 us -> 14.2 us
where the time goes in v1:
time: 597 us; the launch traced here: 592 us
  blocking collectives  213 us (36%)
  waiting for transfers between devices  188 us (31%)
  other arithmetic  108 us (18%)
  local copies, waits for them, and re-layouts  40.4 us (7%)
  matrix products  28 us (5%)
  between operations  14.1 us (2%)
    all_gather x2, blocking collectives, combined_all(): gathered = jax.tree.map(lambda a: lax.all_gather(a, axis), part)  96.7 us
    all_gather x1, waiting for transfers between devices, combined_all(): gathered = jax.tree.map(lambda a: lax.all_gather(a, axis), part)  84.5 us
    all_gather x1, blocking collectives, per_device(): collected = lax.all_gather(drafted[None], ('req', 'mp'), axis=0, tiled=True)  69.3 us
    all_gather x1, waiting for transfers between devices, per_device(): projected = lax.all_gather(own_projection, 'mp', axis=2, tiled=True)  64.1 us
    add x32, other arithmetic, fold_states(): mixed_left * factor_left[..., None] + mixed_right * factor_right[..., None]  54.1 us
    all_gather x1, blocking collectives, per_device(): projected_out = lax.all_gather(out_columns, 'mp', axis=1, tiled=True)  47.5 us
    all_gather x1, waiting for transfers between devices, per_device(): jax.lax.all_gather(jnp.dot(hidden, down_weight, preferred_element_type=jn...  39.2 us
    add x32, other arithmetic, fold_states(): total_left * factor_left + total_right * factor_right  23.7 us
  transfers between devices with their start and end apart: 3, of which 3 were waited for; matrix products, arithmetic and copies ran while one was open for 5% of the time, Pallas kernels for 0%

profile of v1, /device:TPU:8, one launch (start us, length us, event | category | flops | bytes accessed | tf_op | source)
XLA Modules:
  0.0 592.3 jit_solution(13154351890688576730)
XLA Ops:
  7.2 1.7 fusion.81
  13.2 4.8 fusion.77
  18.1 3.9 copy.279
  22.0 4.0 copy.278
  27.2 64.1 %all-gather.9.cloned.1.call-done = bf16[96,3,2048]{0,2,1:T(8,128)(2,1)} async-done(((bf16[96,3,64]{0,2,1:T(8,128)(2,1)}), bf16[96,3,2048]{0,2,1:T(8,128)(2,1)}) %all-gather.9.cloned.1.call-update) | async-done | bytes 1179664 | tf_op jit(solution)/shard_map/all_gather | solution.py:181
  91.3 2.3 slice_convert_fusion.1
  93.6 2.5 copy.240
  103.2 3.5 fusion.80
  107.0 2.4 fusion.20
  109.4 4.4 convolution_bitcast_fusion.1
  115.9 8.8 %fusion.17 = f32[48,16,128,2]{2,3,1,0:T(2,128)} fusion(f32[4,48,16,128]{3,1,2,0:T(8,128)} %convolution_bitcast_fusion.1, pred[4,2]{0,1:T(4,128)(4,1)S(1)} %get-tuple-element.271, f32[2,16,48]{0,1,2:T(8,128)S(1)} %select_reduce_fusion, f32[4,16,48]{0,1,2:T(8,128)S(1)} %copy.246), kind=kOutput, calls=%fused_computation.29 | convolution fusion | flops 9455616 | bytes 2377736 | tf_op jit(solution)/shard_map/prht,pthe->rthe/dot_general | solution.py:130
  124.7 2.8 multiply_reduce_fusion.2
  128.7 2.1 pad_maximum_fusion
  130.8 7.8 %conditional.1 = (f32[2,48,16]{1,2,0:T(8,128)}, f32[2,48,16]{1,2,0:T(8,128)S(1)}, f32[2,48,16,128]{3,2,1,0:T(8,128)S(1)}) conditional(s32[]{:T(128)} %convert_element_type.126, () %tuple.38, (f32[2,48,48]{1,2,0:T(8,128)S(1)}, bf16[96,16,128]{2,1,0:T(8,128)(2,1)}, bf16[2,48,16,128]{3,2,1,0:T(8,128)(2,1)S(1)}, bf16[96,3,2048]{0,2,1:T(8,128)(2,1)}) %tuple.104), branch_computations={%region_9.10_spmd, %region_10.13_spmd} | conditional | flops 38413824 | bytes 8417304 | solution.py:219
  130.8 2.5 copy.250
  134.4 2.0 fusion.76
  139.5 2.5 fusion.26
  142.1 46.7 %all-gather.2 = f32[64,48,16]{1,2,0:T(8,128)S(1)} all-gather(f32[2,48,16]{1,2,0:T(8,128)S(1)} %get-tuple-element.292), channel_id=4, replica_groups=mesh['req'=8,'mp'=32] {'mp'}, dimensions={0}, use_global_device_ids=true | all-gather | bytes 202752 | tf_op jit(solution)/shard_map/all_gather | solution.py:14
  188.8 50.0 %all-gather.1 = f32[64,48,16]{1,2,0:T(8,128)S(1)} all-gather(f32[2,48,16]{1,2,0:T(8,128)S(1)} %get-tuple-element.307), channel_id=3, replica_groups=mesh['req'=8,'mp'=32] {'mp'}, dimensions={0}, use_global_device_ids=true | all-gather | bytes 202752 | tf_op jit(solution)/shard_map/all_gather | solution.py:14
  239.6 84.5 %all-gather.11.cloned.1.call-done = f32[64,48,16,128]{3,2,1,0:T(8,128)} async-done(((f32[2,48,16,128]{3,2,1,0:T(8,128)}), f32[64,48,16,128]{3,2,1,0:T(8,128)}) %all-gather.11.cloned.1.call-update) | async-done | bytes 25165840 | tf_op jit(solution)/shard_map/all_gather | solution.py:14
  325.4 80.2 %while.19 = (s32[]{:T(128)}, f32[2,48,16]{1,2,0:T(8,128)S(1)}, f32[2,48,16]{1,2,0:T(8,128)S(1)}, f32[2,48,16,128]{3,2,1,0:T(8,128)S(1)}, f32[32,2,48,16]{2,3,1,0...) while((s32[]{:T(128)}, f32[2,48,16]{1,2,0:T(8,128)S(1)}, ...), condition=%wide.region_16.17_spmd, body=%wide.region_15.16_spmd.sunk | while | flops 599045 | bytes 2445455 | solution.py:19
  326.3 1.7 fusion.96
  328.9 1.7 fusion.96
  331.4 1.7 fusion.96
  334.0 1.7 fusion.96
  336.6 1.7 fusion.96
  339.2 1.7 fusion.96
  341.8 1.7 fusion.96
  344.4 1.7 fusion.96
  347.0 1.7 fusion.96
  349.6 1.7 fusion.96
  352.1 1.7 fusion.96
  354.7 1.7 fusion.96
  357.3 1.7 fusion.96
  359.9 1.7 fusion.96
  362.5 1.7 fusion.96
  365.1 1.7 fusion.96
  367.7 1.7 fusion.96
  375.4 1.7 fusion.96
  385.8 1.7 fusion.96
  388.3 1.7 fusion.96
  398.7 1.7 fusion.96
  407.2 47.5 %all_gather.41 = bf16[96,2048]{0,1:T(8,128)(2,1)S(1)} all-gather(bf16[96,64]{0,1:T(8,128)(2,1)S(1)} %convolution_convert_fusion.1), channel_id=1, replica_groups=mesh['req'=8,'mp'=32] {'mp'}, dimensions={1}, use_global_device_ids=true | all-gather | bytes 405504 | tf_op jit(solution)/shard_map/all_gather | solution.py:232
  459.8 69.3 %all-gather = bf16[512,4,64]{2,1,0:T(4,128)(2,1)S(1)} all-gather(bf16[2,4,64]{2,1,0:T(4,128)(2,1)S(1)} %add_convert_fusion.1), channel_id=2, replica_groups=mesh['req'=8,'mp'=32] {'req','mp'}, dimensions={0}, use_global_device_ids=true | all-gather | bytes 263168 | tf_op jit(solution)/shard_map/all_gather | solution.py:170
  529.5 2.7 copy.239
  532.2 1.9 convolution_bitcast_fusion.2
  537.0 39.2 %all-gather.13.cloned.1.call-done = bf16[3072,2048]{1,0:T(8,128)(2,1)} async-done(((bf16[96,2048]{1,0:T(8,128)(2,1)}), bf16[3072,2048]{1,0:T(8,128)(2,1)}) %all-gather.13.cloned.1.call-update) | async-done | bytes 12582928 | tf_op jit(solution)/shard_map/all_gather | solution.py:244
  576.2 7.9 %reduce_sum.113 = bf16[96,2048]{1,0:T(8,128)(2,1)S(1)} reduce(bf16[32,96,2048]{2,1,0:T(8,128)(2,1)} %bitcast.130, bf16[]{:T(256)} %constant.157.clone.1), dimensions={0}, to_apply=%region_18.19 | reduce | flops 6094848 | bytes 12976130 | tf_op jit(solution)/shard_map/reduce_sum | solution.py:243
  (222 shorter events, 78.5 us)
Async XLA Ops:
  7.2 448.9 %copy-start = (bf16[2048,2,256]{2,1,0:T(2,128)(2,1)S(1)}, bf16[2048,2,256]{2,1,0:T(2,128)(2,1)}, u32[]{:S(2)}) copy-start(bf16[2048,2,256]{2,1,0:T(2,128)(2,1)} %param.30) | copy-start | bytes 6291460
  7.2 5.2 copy-start.1
  7.2 5.0 copy-start.16
  7.2 84.1 %all-gather.9.cloned.1.call-start = ((), (), s32[]{:S(2)}) async-start(), calls=%async_computation | async-start | bytes 1622016 | tf_op jit(solution)/shard_map/all_gather | solution.py:181
  9.7 314.5 %all-gather.11.cloned.1.call-start = ((), (), s32[]{:S(2)}) async-start(), calls=%async_computation.1 | async-start | bytes 25952256 | tf_op jit(solution)/shard_map/all_gather | solution.py:14
  12.4 5.7 copy-start.17
  12.4 118.4 %copy-start.9 = (f32[2,48,48]{1,2,0:T(8,128)}, f32[2,48,48]{1,2,0:T(8,128)S(1)}, u32[]{:S(2)}) copy-start(f32[2,48,48]{1,2,0:T(8,128)S(1)} %get-tuple-element.315) | copy-start | bytes 55300
  22.0 4.0 copy-start.19
  22.0 4.6 copy-start.12
  97.4 2.9 copy-start.3
  107.0 2.4 copy-start.2
  115.9 8.8 %copy-start.5 = (f32[4,16,48]{0,1,2:T(8,128)S(1)}, f32[4,16,48]{0,1,2:T(8,128)}, u32[]{:S(2)}) copy-start(f32[4,16,48]{0,1,2:T(8,128)} %copy.251) | copy-start | bytes 36868
  142.1 434.1 %all-gather.13.cloned.1.call-start = ((), (), s32[]{:S(2)}) async-start(), calls=%async_computation.2 | async-start | bytes 12976128 | tf_op jit(solution)/shard_map/all_gather | solution.py:244
  238.8 0.8 copy-start.8
  405.9 49.2 %copy-start.4 = (bf16[96,2048]{1,0:T(8,128)(2,1)S(1)}, bf16[96,2048]{1,0:T(8,128)(2,1)}, u32[]{:S(2)}) copy-start(bf16[96,2048]{1,0:T(8,128)(2,1)} %param.21) | copy-start | bytes 1179652
  405.9 49.2 %copy-start.13 = (f32[1,2048]{1,0:T(1,128)S(1)}, f32[1,2048]{1,0:T(1,128)}, u32[]{:S(2)}) copy-start(f32[1,2048]{1,0:T(1,128)} %get-tuple-element.308) | copy-start | bytes 24580
  455.3 0.7 copy-start.11
  456.0 1.2 copy-start.6
  457.3 1.9 copy-start.15
  457.3 2.0 copy-start.7
  532.2 2.6 copy-start.20
  532.2 2.6 copy-start.10
  532.2 4.0 copy-start.18
  576.2 8.0 %copy-start.14 = (f32[1,2048]{1,0:T(1,128)S(1)}, f32[1,2048]{1,0:T(1,128)}, u32[]{:S(2)}) copy-start(f32[1,2048]{1,0:T(1,128)} %get-tuple-element.311) | copy-start | bytes 24580
Sparse Core Ops, SparseCore 0:
  11.2 80.0 all-gather.8
  142.2 181.9 all-gather.10
  458.5 117.6 all-gather.12
